TPU v7x, 32 devices: a whole 2x2x4 slice. The times are simulated.
32 devices in a mesh: area: 8 (over z, x), unit: 4 (over y, core).
Axes of the slice: x: 2, y: 2, z: 4, core: 2. Of those that a mesh axis runs over, the one named last changes fastest.
Arguments:
- initial_rates: float32 [8, 4096, 128], P('area', 'unit'), may hold values from -0.9 to 0.9
- prior_rates: bfloat16 [8, 4096, 128], P('area', 'unit'), may hold values from -0.8984375 to 0.8984375
- local_weight: bfloat16 [8, 4096, 4096], P('area', 'unit'), may hold values from -0.125 to 0.125
- long_weight: bfloat16 [8, 4096, 2048], P('area', 'unit'), may hold values from -0.1875 to 0.1875
- input_weight: bfloat16 [8, 4096, 16], P('area', 'unit'), may hold values from -1.5 to 1.5
- unit_bias: float32 [8, 4096], P('area', 'unit'), may hold values from -2.5 to 2.5
- leak_rate: float32 [8, 4096], P('area', 'unit'), may hold values from 0.2 to 1
- stimulus: bfloat16 [6, 16, 128], replicated, may hold values from -4 to 4
- link_source: int32 [8, 16], replicated, may hold values from 0 to 7, as said below
- link_block: int32 [8, 16], replicated, may hold values from 0 to 31
- link_delay: int32 [8, 16], replicated, may hold values from 0 to 1
Outputs:
- final_rates: float32 [8, 4096, 128], P('area', 'unit')
- final_current: float32 [8, 4096, 128], P('area', 'unit')
Inputs may be any that keep to these rules, and one draw needn't show every extreme that they name: `link_source`: each area's 16 entries name every source area at most 2 times, and some source area exactly 2 times.
All inputs are finite; a program needn't handle non-finite values.
Results may differ from a plain program's by a relative error of at most 0.004.
Values may be sent and summed in bfloat16 or wider, within the bound.
A program may use at most 64 MiB of HBM per device.

v0:
```python
import functools

import jax
import jax.numpy as jnp
from jax import lax
from jax.experimental import pallas as pl
from jax.experimental.pallas import tpu as pltpu
from jax.sharding import PartitionSpec as P

BLOCK = 128
HALF = BLOCK // 2
WINDOWS = 3
CORES = 2
CHUNKS = 2
EXCHANGES = WINDOWS + 1
GENERATIONS = 2 * EXCHANGES


def kernel(n_area, n_unit, per_pair, slots, *refs):
    (send_block, send_delay, take_rows, start_ref, prior_ref, local_hbm, long_hbm,
     input_ref, bias_ref, leak_ref, stim_ref, rates, current) = refs[:13]
    full = refs[13 : 13 + GENERATIONS]
    inbox = refs[13 + GENERATIONS : 13 + GENERATIONS + EXCHANGES]
    (local_w, long_w, outbox, inputs, drive, weight_sem, share_send, share_recv,
     block_send, block_recv, pass_send, pass_recv) = refs[13 + GENERATIONS + EXCHANGES :]
    rows, trials = rates.shape
    chips = n_unit // CORES
    shard = rows // HALF
    part = shard // CHUNKS
    tile = rows // CHUNKS
    area, unit = lax.axis_index("area"), lax.axis_index("unit")
    chip, core = unit // CORES, unit % CORES
    sibling = chip * CORES + (1 - core)

    def chip_at(offset):
        return lax.rem(chip + offset + chips, chips)

    def area_at(offset):
        return lax.rem(area + offset + n_area, n_area)

    loads = [
        pltpu.make_async_copy(
            local_hbm.at[:, pl.ds(u * rows, rows)], local_w.at[u], weight_sem.at[u]
        )
        for u in range(n_unit)
    ]
    loads.append(pltpu.make_async_copy(long_hbm, long_w, weight_sem.at[n_unit]))
    for load in loads:
        load.start()

    barrier = pltpu.get_barrier_semaphore()
    pl.semaphore_signal(barrier, inc=1, device_id={"unit": sibling})
    for j in range(1, chips):
        pl.semaphore_signal(barrier, inc=1, device_id={"unit": chip_at(j) * CORES + core})

    @pl.loop(1, n_area)
    def _(d):
        pl.semaphore_signal(barrier, inc=1, device_id={"area": area_at(d)})

    pl.semaphore_wait(barrier, 1 + (chips - 1) + (n_area - 1))

    def share(g, k, lane):
        if lane == 0:
            owner, target = unit, sibling
        elif lane < chips:
            owner, target = unit, chip_at(lane) * CORES + core
        else:
            owner, target = chip_at(-(lane - chips + 1)) * CORES + core, sibling
        place = full[g].at[pl.ds(owner * shard + k * part, part)]
        return pltpu.make_async_remote_copy(
            src_ref=place,
            dst_ref=place,
            send_sem=share_send.at[g % 2, k, lane],
            recv_sem=share_recv.at[g, k, lane],
            device_id={"unit": target},
        )

    lanes = 2 * chips - 1

    def share_out(g, k):
        for lane in range(1, chips):
            share(g, k, lane).start()
        share(g, k, 0).start()

    def hand_on(g):
        for k in range(CHUNKS):
            for j in range(1, chips):
                share(g, k, j).wait_recv()
                share(g, k, chips - 1 + j).start()

    def wait_lane(g, lane):
        for k in range(CHUNKS):
            share(g, k, lane).wait_recv()

    def sends_done(g):
        for k in range(CHUNKS):
            for lane in range(lanes):
                share(g, k, lane).wait_send()

    def copy_of(g, owner):
        return full[g][pl.ds(owner * shard, shard)].reshape(rows, trials)

    def product(g, owner, at):
        return jnp.dot(local_w[owner, at, :], copy_of(g, owner), preferred_element_type=jnp.float32)

    def span(k):
        return pl.ds(pl.multiple_of(k * tile, tile), tile)

    def begin(g, n):
        @pl.loop(0, CHUNKS)
        def _(k):
            at = span(k)
            given = jnp.dot(input_ref[at, :], stim_ref[n], preferred_element_type=jnp.float32)
            drive[at, :] = product(g, unit, at) + given + bias_ref[at, :]

    def add(g, owner):
        @pl.loop(0, CHUNKS)
        def _(k):
            at = span(k)
            drive[at, :] += product(g, owner, at)

    def long_product(at):
        return jnp.dot(
            long_w[at, :], inputs[...].reshape(slots * BLOCK, trials),
            preferred_element_type=jnp.float32,
        )

    def settle(g, k, total):
        at = pl.ds(k * tile, tile)
        old = rates[at, :]
        new = old + leak_ref[at, :] * (jnp.tanh(total) - old)
        rates[at, :] = new
        full[g + 1][pl.ds(unit * shard + k * part, part)] = new.astype(jnp.bfloat16).reshape(
            part, HALF, trials
        )
        share_out(g + 1, k)

    def pick(e, entry, half):
        where = send_block[entry] * 2 + half
        earlier, later = full[2 * e][where], full[2 * e + 1][where]
        return jnp.where(send_delay[entry] == 0, later, earlier)

    def outgoing(e, d):
        target = area_at(d)
        return pltpu.make_async_remote_copy(
            src_ref=outbox.at[pl.ds(target * per_pair, per_pair)],
            dst_ref=inbox[e].at[core, pl.ds(area * per_pair, per_pair)],
            send_sem=block_send.at[d],
            recv_sem=block_recv.at[e, d],
            device_id={"area": target},
        )

    def passing(e, d):
        place = inbox[e].at[core, pl.ds(area_at(-d) * per_pair, per_pair)]
        return pltpu.make_async_remote_copy(
            src_ref=place,
            dst_ref=place,
            send_sem=pass_send.at[d],
            recv_sem=pass_recv.at[e, d],
            device_id={"unit": sibling},
        )

    def send_blocks(e):
        @pl.loop(1, n_area)
        def _(d):
            for p in range(per_pair):
                entry = area_at(d) * per_pair + p
                outbox[entry] = pick(e, entry, core)
            outgoing(e, d).start()

        for p in range(per_pair):
            entry = area * per_pair + p
            for half in range(2):
                inbox[e][half, entry] = pick(e, entry, half)

    def take_blocks(e):
        @pl.loop(1, n_area)
        def _(d):
            outgoing(e, d).wait_recv()
            passing(e, d).start()

        @pl.loop(1, n_area)
        def _(d):
            passing(e, d).wait_recv()
            passing(e, d).wait_send()
            outgoing(e, d).wait_send()

        @pl.loop(0, slots)
        def _(slot):
            for half in range(2):
                inputs[slot * 2 + half] = inbox[e][half, take_rows[slot]]

    away = [(chip_at(-j), chips - 1 + j) for j in range(1, chips)]

    rates[...] = start_ref[...]
    own = pl.ds(unit * shard, shard)
    full[1][own] = start_ref[...].astype(jnp.bfloat16).reshape(shard, HALF, trials)
    full[0][own] = prior_ref[...].reshape(shard, HALF, trials)
    for g in (1, 0):
        for k in range(CHUNKS):
            share_out(g, k)
    for load in loads:
        load.wait()

    for step in range(2 * WINDOWS):
        g = step + 1
        begin(g, step)
        wait_lane(g, 0)
        add(g, sibling)
        hand_on(g)
        if step == 0:
            hand_on(0)
            for lane in [0] + [lane for _, lane in away]:
                wait_lane(0, lane)
            sends_done(0)
        if step % 2 == 0:
            for _, lane in away:
                wait_lane(g, lane)
            send_blocks(step // 2)
            for source, _ in away:
                add(g, source * CORES + core)
                add(g, source * CORES + (1 - core))
            take_blocks(step // 2)
            for k in range(CHUNKS):
                at = pl.ds(k * tile, tile)
                now = long_product(at)
                current[at, :] = now
                settle(g, k, drive[at, :] + now)
        else:
            for source, _ in away:
                add(g, source * CORES + core)
            for source, lane in away[:-1]:
                wait_lane(g, lane)
                add(g, source * CORES + (1 - core))
            source, lane = away[-1]
            wait_lane(g, lane)
            for k in range(CHUNKS):
                at = pl.ds(k * tile, tile)
                total = drive[at, :] + product(g, source * CORES + (1 - core), at)
                settle(g, k, total + current[at, :])
        sends_done(g)

    g = GENERATIONS - 1
    wait_lane(g, 0)
    hand_on(g)
    for _, lane in away:
        wait_lane(g, lane)
    send_blocks(WINDOWS)
    take_blocks(WINDOWS)
    for k in range(CHUNKS):
        at = pl.ds(k * tile, tile)
        current[at, :] = long_product(at)
    sends_done(g)


def shards(
    initial_rates,
    prior_rates,
    local_weight,
    long_weight,
    input_weight,
    unit_bias,
    leak_rate,
    stimulus,
    link_source,
    link_block,
    link_delay,
):
    areas_all, slot_count = link_source.shape
    per_pair = max(1, -(-slot_count // areas_all))
    n_area, n_unit = lax.axis_size("area"), lax.axis_size("unit")
    area_here = lax.axis_index("area")
    slot_order = jnp.arange(slot_count, dtype=jnp.int32)
    same_source = (link_source[:, :, None] == link_source[:, None, :]) & (
        slot_order[None, None, :] < slot_order[None, :, None]
    )
    pair_index = jnp.sum(same_source.astype(jnp.int32), axis=2)
    from_here = link_source == area_here
    pair_range = jnp.arange(per_pair, dtype=jnp.int32)
    matched = from_here[:, None, :] & (pair_index[:, None, :] == pair_range[None, :, None])
    send_block = jnp.sum(jnp.where(matched, link_block[:, None, :], 0), axis=2).reshape(-1)
    send_delay = jnp.sum(jnp.where(matched, link_delay[:, None, :], 0), axis=2).reshape(-1)
    own_source = lax.dynamic_index_in_dim(link_source, area_here, 0, keepdims=False)
    own_pair = lax.dynamic_index_in_dim(pair_index, area_here, 0, keepdims=False)
    take_rows = own_source * per_pair + own_pair

    rows, trials = initial_rates.shape[1:]
    units = local_weight.shape[2]
    pairs = areas_all * per_pair
    lanes = 2 * (n_unit // CORES) - 1
    smem = pl.BlockSpec(memory_space=pltpu.SMEM)
    vmem = pl.BlockSpec(memory_space=pltpu.VMEM)
    far = pl.BlockSpec(memory_space=pl.ANY)
    half_blocks = units // HALF
    dma = pltpu.SemaphoreType.DMA
    out = jax.ShapeDtypeStruct((rows, trials), jnp.float32)
    rates, current = pl.pallas_call(
        functools.partial(kernel, n_area, n_unit, per_pair, slot_count),
        out_shape=(out, out),
        in_specs=[smem] * 3 + [vmem] * 2 + [far] * 2 + [vmem] * 4,
        out_specs=(vmem, vmem),
        scratch_shapes=[pltpu.VMEM((half_blocks, HALF, trials), jnp.bfloat16)] * GENERATIONS
        + [pltpu.VMEM((2, pairs, HALF, trials), jnp.bfloat16)] * EXCHANGES
        + [
            pltpu.VMEM((n_unit, rows, rows), jnp.bfloat16),
            pltpu.VMEM((rows, slot_count * BLOCK), jnp.bfloat16),
            pltpu.VMEM((pairs, HALF, trials), jnp.bfloat16),
            pltpu.VMEM((2 * slot_count, HALF, trials), jnp.bfloat16),
            pltpu.VMEM((rows, trials), jnp.float32),
            dma((n_unit + 1,)),
            dma((2, CHUNKS, lanes)),
            dma((GENERATIONS, CHUNKS, lanes)),
            dma((n_area,)),
            dma((EXCHANGES, n_area)),
            dma((n_area,)),
            dma((EXCHANGES, n_area)),
        ],
        compiler_params=pltpu.CompilerParams(
            collective_id=0, has_side_effects=True, vmem_limit_bytes=48 * 2**20
        ),
    )(
        send_block, send_delay, take_rows, initial_rates[0], prior_rates[0],
        local_weight[0], long_weight[0], input_weight[0], unit_bias[0][:, None],
        leak_rate[0][:, None], stimulus,
    )
    return (rates[None], current[None])


def solution(mesh):
    return jax.shard_map(
        shards,
        mesh=mesh,
        in_specs=(
            P("area", "unit", None),
            P("area", "unit", None),
            P("area", "unit", None),
            P("area", "unit", None),
            P("area", "unit", None),
            P("area", "unit"),
            P("area", "unit"),
            P(),
            P(),
            P(),
            P(),
        ),
        out_specs=(P("area", "unit", None), P("area", "unit", None)),
        check_vma=False,
    )
```

profile of v0, /device:TPU:0, one launch (start us, length us, event | category | flops | bytes accessed | tf_op | source)
XLA Modules:
  0.0 126.5 jit_solution(12343223532709154363)
XLA Ops:
  0.6 0.7 broadcast_compare_fusion
  1.3 1.0 convert_reduce_fusion
  2.4 0.7 add_bitcast_fusion.refs_2_
  3.1 0.8 select_reduce_fusion
  3.9 0.1 copy.18
  4.0 0.1 reshape.35.refs_1_
  4.1 0.1 copy.17
  4.2 0.1 reshape.34.refs_0_
  4.3 0.9 copy.19
  5.2 0.9 copy.20.refs_8_
  6.1 0.9 copy.21.refs_9_
  7.0 0.0 copy-start
  7.0 1.0 copy-done
  8.1 0.0 copy-start.1
  8.1 0.9 copy-done.1
  9.0 0.0 copy-start.2
  9.0 0.7 copy-done.2
  9.8 115.1 %shard_map.122 = (f32[1024,128]{1,0:T(8,128)S(1)}, f32[1024,128]{1,0:T(8,128)S(1)}) custom-call(s32[16]{0:T(128)S(1)} %reshape.34.refs_0_, s32[16]{0:T(128)S(1)} %reshape.35.refs_1_, s32[16]{0:T(128)S(1)} %add_bitcast_fusion.refs_2_, f32[1024,128]{1,0:T(8,128)S(1)} %bitcast.12, bf16[1024,128]{1,0:T(8,128)(2,1)S(1)} %bitcast.15, bf16[1024,4096]{1,0:T(8,128)(2,1)} %bitcast.16, ...), custom_call_target="tpu_custom_call" | custom-call | tf_op jit(solution)/shard_map/pallas_call | solution.py:297
  124.9 0.8 copy.24
  125.7 0.8 copy.25
  (1 shorter events, 0.0 us)
Async XLA Ops:
  7.0 1.0 copy-start
  8.1 0.9 copy-start.1
  9.0 0.7 copy-start.2
where the time goes:
time: 127 us; the launch traced here: 126 us
  Pallas kernels  115 us (91%)
  local copies, waits for them, and re-layouts  7.39 us (6%)
  other arithmetic  3.29 us (3%)
    pallas_call x1, Pallas kernels, shards(): pl.pallas_call(functools.partial(kernel, n_area, n_unit, per_pair, slot_c...  115 us
    unnamed x9, local copies, waits for them, and re-layouts  5.25 us

commit v1 on v0

--- a/solution.py
+++ b/solution.py
@@ -11,7 +11,8 @@
 HALF = BLOCK // 2
 WINDOWS = 3
 CORES = 2
-CHUNKS = 2
+CHUNKS = 4
+TILES = 2
 EXCHANGES = WINDOWS + 1
 GENERATIONS = 2 * EXCHANGES
 
@@ -27,7 +28,8 @@
     chips = n_unit // CORES
     shard = rows // HALF
     part = shard // CHUNKS
-    tile = rows // CHUNKS
+    tile = rows // TILES
+    band = rows // CHUNKS
     area, unit = lax.axis_index("area"), lax.axis_index("unit")
     chip, core = unit // CORES, unit % CORES
     sibling = chip * CORES + (1 - core)
@@ -107,14 +109,14 @@
         return pl.ds(pl.multiple_of(k * tile, tile), tile)
 
     def begin(g, n):
-        @pl.loop(0, CHUNKS)
+        @pl.loop(0, TILES)
         def _(k):
             at = span(k)
             given = jnp.dot(input_ref[at, :], stim_ref[n], preferred_element_type=jnp.float32)
             drive[at, :] = product(g, unit, at) + given + bias_ref[at, :]
 
     def add(g, owner):
-        @pl.loop(0, CHUNKS)
+        @pl.loop(0, TILES)
         def _(k):
             at = span(k)
             drive[at, :] += product(g, owner, at)
@@ -126,7 +128,7 @@
         )
 
     def settle(g, k, total):
-        at = pl.ds(k * tile, tile)
+        at = pl.ds(k * band, band)
         old = rates[at, :]
         new = old + leak_ref[at, :] * (jnp.tanh(total) - old)
         rates[at, :] = new
@@ -222,7 +224,7 @@
                 add(g, source * CORES + (1 - core))
             take_blocks(step // 2)
             for k in range(CHUNKS):
-                at = pl.ds(k * tile, tile)
+                at = pl.ds(k * band, band)
                 now = long_product(at)
                 current[at, :] = now
                 settle(g, k, drive[at, :] + now)
@@ -235,7 +237,7 @@
             source, lane = away[-1]
             wait_lane(g, lane)
             for k in range(CHUNKS):
-                at = pl.ds(k * tile, tile)
+                at = pl.ds(k * band, band)
                 total = drive[at, :] + product(g, source * CORES + (1 - core), at)
                 settle(g, k, total + current[at, :])
         sends_done(g)
@@ -248,7 +250,7 @@
     send_blocks(WINDOWS)
     take_blocks(WINDOWS)
     for k in range(CHUNKS):
-        at = pl.ds(k * tile, tile)
+        at = pl.ds(k * band, band)
         current[at, :] = long_product(at)
     sends_done(g)
 

time: 127 us -> 124 us (0.976)
  Pallas kernels: 115 us -> 112 us
    pallas_call x1, Pallas kernels: 115 us -> 112 us  [shards(): pl.pallas_call(functools.partial(kernel, n_area, n_unit, per_pair, slot_c...]
where the time goes in v1:
time: 124 us; the launch traced here: 123 us
  Pallas kernels  112 us (90%)
  local copies, waits for them, and re-layouts  7.39 us (6%)
  other arithmetic  3.29 us (3%)
    pallas_call x1, Pallas kernels, shards(): pl.pallas_call(functools.partial(kernel, n_area, n_unit, per_pair, slot_c...  112 us
    unnamed x9, local copies, waits for them, and re-layouts  5.25 us

profile of v1, /device:TPU:0, one launch (start us, length us, event | category | flops | bytes accessed | tf_op | source)
XLA Modules:
  0.0 123.0 jit_solution(1201042287225979398)
XLA Ops:
  0.6 0.7 broadcast_compare_fusion
  1.3 1.0 convert_reduce_fusion
  2.4 0.7 add_bitcast_fusion.refs_2_
  3.1 0.8 select_reduce_fusion
  3.9 0.1 copy.18
  4.0 0.1 reshape.35.refs_1_
  4.1 0.1 copy.17
  4.2 0.1 reshape.34.refs_0_
  4.3 0.9 copy.19
  5.2 0.9 copy.20.refs_8_
  6.1 0.9 copy.21.refs_9_
  7.0 0.0 copy-start
  7.0 1.0 copy-done
  8.1 0.0 copy-start.1
  8.1 0.9 copy-done.1
  9.0 0.0 copy-start.2
  9.0 0.7 copy-done.2
  9.8 111.7 %shard_map.122 = (f32[1024,128]{1,0:T(8,128)S(1)}, f32[1024,128]{1,0:T(8,128)S(1)}) custom-call(s32[16]{0:T(128)S(1)} %reshape.34.refs_0_, s32[16]{0:T(128)S(1)} %reshape.35.refs_1_, s32[16]{0:T(128)S(1)} %add_bitcast_fusion.refs_2_, f32[1024,128]{1,0:T(8,128)S(1)} %bitcast.12, bf16[1024,128]{1,0:T(8,128)(2,1)S(1)} %bitcast.15, bf16[1024,4096]{1,0:T(8,128)(2,1)} %bitcast.16, ...), custom_call_target="tpu_custom_call" | custom-call | tf_op jit(solution)/shard_map/pallas_call | solution.py:299
  121.5 0.8 copy.24
  122.3 0.8 copy.25
  (1 shorter events, 0.0 us)
Async XLA Ops:
  7.0 1.0 copy-start
  8.1 0.9 copy-start.1
  9.0 0.7 copy-start.2

commit v2 on v1

--- a/solution.py
+++ b/solution.py
@@ -40,6 +40,11 @@
     def area_at(offset):
         return lax.rem(area + offset + n_area, n_area)
 
+    own = pl.ds(unit * shard, shard)
+    states = [
+        pltpu.make_async_copy(start_ref, rates, weight_sem.at[n_unit + 1]),
+        pltpu.make_async_copy(prior_ref, full[0].at[own], weight_sem.at[n_unit + 2]),
+    ]
     loads = [
         pltpu.make_async_copy(
             local_hbm.at[:, pl.ds(u * rows, rows)], local_w.at[u], weight_sem.at[u]
@@ -47,7 +52,7 @@
         for u in range(n_unit)
     ]
     loads.append(pltpu.make_async_copy(long_hbm, long_w, weight_sem.at[n_unit]))
-    for load in loads:
+    for load in states + loads:
         load.start()
 
     barrier = pltpu.get_barrier_semaphore()
@@ -194,10 +199,9 @@
 
     away = [(chip_at(-j), chips - 1 + j) for j in range(1, chips)]
 
-    rates[...] = start_ref[...]
-    own = pl.ds(unit * shard, shard)
-    full[1][own] = start_ref[...].astype(jnp.bfloat16).reshape(shard, HALF, trials)
-    full[0][own] = prior_ref[...].reshape(shard, HALF, trials)
+    for load in states:
+        load.wait()
+    full[1][own] = rates[...].astype(jnp.bfloat16).reshape(shard, HALF, trials)
     for g in (1, 0):
         for k in range(CHUNKS):
             share_out(g, k)
@@ -299,7 +303,7 @@
     rates, current = pl.pallas_call(
         functools.partial(kernel, n_area, n_unit, per_pair, slot_count),
         out_shape=(out, out),
-        in_specs=[smem] * 3 + [vmem] * 2 + [far] * 2 + [vmem] * 4,
+        in_specs=[smem] * 3 + [far] * 4 + [vmem] * 4,
         out_specs=(vmem, vmem),
         scratch_shapes=[pltpu.VMEM((half_blocks, HALF, trials), jnp.bfloat16)] * GENERATIONS
         + [pltpu.VMEM((2, pairs, HALF, trials), jnp.bfloat16)] * EXCHANGES
@@ -309,7 +313,7 @@
             pltpu.VMEM((pairs, HALF, trials), jnp.bfloat16),
             pltpu.VMEM((2 * slot_count, HALF, trials), jnp.bfloat16),
             pltpu.VMEM((rows, trials), jnp.float32),
-            dma((n_unit + 1,)),
+            dma((n_unit + 3,)),
             dma((2, CHUNKS, lanes)),
             dma((GENERATIONS, CHUNKS, lanes)),
             dma((n_area,)),
@@ -318,10 +322,11 @@
             dma((EXCHANGES, n_area)),
         ],
         compiler_params=pltpu.CompilerParams(
-            collective_id=0, has_side_effects=True, vmem_limit_bytes=48 * 2**20
+            collective_id=0, has_side_effects=True, vmem_limit_bytes=56 * 2**20
         ),
     )(
-        send_block, send_delay, take_rows, initial_rates[0], prior_rates[0],
+        send_block, send_delay, take_rows, initial_rates[0],
+        prior_rates[0].reshape(rows // HALF, HALF, trials),
         local_weight[0], long_weight[0], input_weight[0], unit_bias[0][:, None],
         leak_rate[0][:, None], stimulus,
     )

time: 124 us -> 129 us (1.040)
  local copies, waits for them, and re-layouts: 7.39 us -> 10.2 us
    pallas_call x1, Pallas kernels: 112 us -> 113 us  [shards(): pl.pallas_call(functools.partial(kernel, n_area, n_unit, per_pair, slot_c...]
    unnamed x9 -> x3, local copies, waits for them, and re-layouts: 5.25 us -> 5.35 us
where the time goes in v2:
time: 129 us; the launch traced here: 128 us
  Pallas kernels  113 us (88%)
  local copies, waits for them, and re-layouts  10.2 us (8%)
  other arithmetic  3.87 us (3%)
    pallas_call x1, Pallas kernels, shards(): pl.pallas_call(functools.partial(kernel, n_area, n_unit, per_pair, slot_c...  113 us
    unnamed x3, local copies, waits for them, and re-layouts  5.35 us

profile of v2, /device:TPU:0, one launch (start us, length us, event | category | flops | bytes accessed | tf_op | source)
XLA Modules:
  0.0 128.1 jit_solution(6371657694267287371)
XLA Ops:
  0.6 0.7 broadcast_compare_fusion
  1.3 1.0 convert_reduce_fusion
  2.4 1.3 add_bitcast_fusion.refs_2_
  3.7 0.8 select_reduce_fusion
  4.5 0.1 copy.18
  4.6 0.6 reshape.35.refs_1_
  5.2 0.1 copy.17
  5.3 0.6 reshape.34.refs_0_
  5.9 1.6 %copy.19 = bf16[1,1024,16]{2,1,0:T(8,128)(2,1)} copy(bf16[1,1024,16]{1,2,0:T(8,128)(2,1)} %param.15) | data formatting | bytes 65536 | tf_op args[4]
  7.5 1.7 %copy.20.refs_8_ = f32[1024,1]{1,0:T(8,128)} copy(f32[1024,1]{0,1:T(1,128)} %bitcast.18) | data formatting | bytes 8192 | tf_op jit(solution)/shard_map/broadcast_in_dim;squeeze | solution.py:330
  9.2 1.7 %copy.21.refs_9_ = f32[1024,1]{1,0:T(8,128)} copy(f32[1024,1]{0,1:T(1,128)} %bitcast.19) | data formatting | bytes 8192 | tf_op jit(solution)/shard_map/broadcast_in_dim;squeeze | solution.py:331
  10.9 113.4 %shard_map.122 = (f32[1024,128]{1,0:T(8,128)}, f32[1024,128]{1,0:T(8,128)}) custom-call(s32[16]{0:T(128)} %reshape.34.refs_0_, s32[16]{0:T(128)} %reshape.35.refs_1_, s32[16]{0:T(128)} %add_bitcast_fusion.refs_2_, f32[1024,128]{1,0:T(8,128)} %bitcast.14, bf16[16,64,128]{2,1,0:T(8,128)(2,1)} %bitcast.17, bf16[1024,4096]{1,0:T(8,128)(2,1)} %bitcast.11, ...), custom_call_target="tpu_custom_call" | custom-call | tf_op jit(solution)/shard_map/pallas_call | solution.py:303
  124.3 1.9 %copy.24 = f32[1,1024,128]{2,1,0:T(8,128)} copy(f32[1,1024,128]{2,1,0:T(8,128)} %bitcast.16) | data formatting | bytes 1048576
  126.2 1.9 %copy.25 = f32[1,1024,128]{2,1,0:T(8,128)} copy(f32[1,1024,128]{2,1,0:T(8,128)} %bitcast.15) | data formatting | bytes 1048576
  (1 shorter events, 0.0 us)
